TPU v7x, 512 devices: a whole 4x4x16 slice. The times are simulated.
512 devices in a mesh: tm: 32 (over x, y, core), panel: 16 (over z).
Axes of the slice: x: 4, y: 4, z: 16, core: 2. Of those that a mesh axis runs over, the one named last changes fastest.
Arguments:
- elem_trans: float32 [32, 1024, 1024], P('tm', 'panel'), may hold values from -0.1875 to 0.1875
- elem_cov: float32 [32, 1024, 1024], P('tm', 'panel'), may hold values from -1 to 12, as said below
- elem_info: float32 [32, 1024, 1024], P('tm', 'panel'), may hold values from -1 to 8, as said below
- elem_mean: float32 [32, 1024], P('tm', 'panel'), may hold values from -6 to 6
- elem_infovec: float32 [32, 1024], P('tm', 'panel'), may hold values from -6 to 6
Outputs:
- new_cov: float32 [32, 1024, 1024], P('tm', 'panel')
- new_mean: float32 [32, 1024], P('tm', 'panel')
Inputs may be any that keep to these rules, and one draw needn't show every extreme that they name: `elem_cov`: each group's matrix is symmetric positive definite. `elem_info`: each group's matrix is symmetric positive definite.
All inputs are finite; a program needn't handle non-finite values.
Results may differ from a plain program's by a relative error of at most 0.000064.
Values sent between devices are 32-bit elements; how exact they have to be, the bound alone decides.
A program may use at most 128 MiB of HBM per device.

v0:
```python
import jax
import jax.numpy as jnp
from jax import lax
from jax.sharding import PartitionSpec as P

HIGHEST = lax.Precision.HIGHEST


def from_behind(array, axis, by):
    devices = lax.axis_size(axis)
    pairs = [(i, i + by) for i in range(devices) if 0 <= i + by < devices]
    return lax.ppermute(array, axis, pairs)


def block_cholesky(matrix):
    state_count = matrix.shape[0]
    split = state_count // 2
    top_left = matrix[:split, :split]
    bottom_left = matrix[split:, :split]
    bottom_right = matrix[split:, split:]
    first_factor = jnp.linalg.cholesky(top_left)
    side_block = jax.scipy.linalg.solve_triangular(first_factor, bottom_left.T, lower=True).T
    schur_block = bottom_right - jnp.dot(side_block, side_block.T, precision=HIGHEST)
    second_factor = jnp.linalg.cholesky(schur_block)
    upper_rows = jnp.concatenate(
        [first_factor, jnp.zeros((split, state_count - split), jnp.float32)], axis=1
    )
    lower_rows = jnp.concatenate([side_block, second_factor], axis=1)
    return jnp.concatenate([upper_rows, lower_rows], axis=0)


def body(elem_trans, elem_cov, elem_info, elem_mean, elem_infovec):
    distance = lax.axis_size("tm") // 2
    transition = elem_trans[0]
    covariance = elem_cov[0]
    information = elem_info[0]
    state_mean = elem_mean[0]
    info_vector = elem_infovec[0]
    state_count = covariance.shape[1]
    upper = lax.axis_index("tm") >= distance
    identity_matrix = jnp.eye(state_count, dtype=jnp.float32)
    prev_cov, prev_mean = from_behind((covariance, state_mean), "tm", distance)
    whole_cov, whole_mean = (
        lax.all_gather(prev_cov, "panel", axis=0, tiled=True),
        lax.all_gather(prev_mean, "panel", axis=0, tiled=True),
    )
    whole_cov = jnp.where(upper, whole_cov, identity_matrix)
    lower_factor = block_cholesky(whole_cov)
    coupling_rows = jnp.dot(information, lower_factor, precision=HIGHEST)
    coupling, whole_vector = (
        lax.all_gather(coupling_rows, "panel", axis=0, tiled=True),
        lax.all_gather(info_vector, "panel", axis=0, tiled=True),
    )
    inner = identity_matrix + jnp.dot(lower_factor.T, coupling, precision=HIGHEST)
    inner_factor = block_cholesky(inner)
    mixed_rows = jnp.dot(transition, lower_factor, precision=HIGHEST)
    factor_part = jax.scipy.linalg.solve_triangular(inner_factor, mixed_rows.T, lower=True).T
    combined_rows = (
        jnp.dot(
            factor_part,
            lax.all_gather(factor_part, "panel", axis=0, tiled=True).T,
            precision=HIGHEST,
        )
        + covariance
    )
    right_side = jax.scipy.linalg.solve_triangular(lower_factor, whole_mean, lower=True)
    right_side = right_side + jnp.dot(whole_vector, lower_factor, precision=HIGHEST)
    weight = jax.scipy.linalg.cho_solve((inner_factor, True), right_side)
    combined_mean = jnp.dot(mixed_rows, weight, precision=HIGHEST) + state_mean
    result_cov = jnp.where(upper, combined_rows, covariance)
    result_mean = jnp.where(upper, combined_mean, state_mean)
    return (result_cov[None], result_mean[None])


def solution(mesh):
    return jax.shard_map(
        body,
        mesh=mesh,
        in_specs=(
            P("tm", "panel", None),
            P("tm", "panel", None),
            P("tm", "panel", None),
            P("tm", "panel"),
            P("tm", "panel"),
        ),
        out_specs=(P("tm", "panel", None), P("tm", "panel")),
        check_vma=False,
    )
```

profile of v0, /device:TPU:1, one launch (start us, length us, event | category | flops | bytes accessed | tf_op | source)
XLA Modules:
  0.0 1011.7 jit_solution(16703277479244378389)
XLA Ops:
  7.2 5.6 collective-permute-start
  12.9 3.6 collective-permute-done
  17.3 77.9 %all-gather.5.cloned.1.call-done = f32[1024,1024]{1,0:T(8,128)} async-done(((f32[64,1024]{1,0:T(8,128)}), f32[1024,1024]{1,0:T(8,128)}) %all-gather.5.cloned.1.call-update) | async-done | bytes 4194320 | tf_op jit(solution)/shard_map/all_gather | solution.py:44
  95.1 5.3 copy.31
  105.9 11.7 %cholesky.462 = f32[128,128]{1,0:T(8,128)S(1)} custom-call(f32[128,128]{1,0:T(8,128)S(1)} %cholesky.746), custom_call_target="Cholesky" | custom-call | tf_op jit(solution)/shard_map/jit(cholesky)/cholesky | solution.py:21
  117.6 9.8 custom-call.45
  128.9 11.7 %cholesky.481 = f32[128,128]{1,0:T(8,128)S(1)} custom-call(f32[128,128]{1,0:T(8,128)S(1)} %cholesky.750), custom_call_target="Cholesky" | custom-call | tf_op jit(solution)/shard_map/jit(cholesky)/cholesky | solution.py:21
  140.6 10.0 custom-call.46
  152.9 13.2 %cholesky.502 = f32[128,128]{1,0:T(8,128)} custom-call(f32[128,128]{1,0:T(8,128)} %cholesky.755), custom_call_target="Cholesky" | custom-call | tf_op jit(solution)/shard_map/jit(cholesky)/cholesky | solution.py:21
  168.2 11.3 %custom-call.47 = f32[1,128,128]{1,2,0:T(8,128)} custom-call(f32[1,128,128]{2,1,0:T(8,128)} %get-tuple-element.130), custom_call_target="InvertDiagBlocksLowerTriangular" | custom-call | tf_op jit(solution)/shard_map/jit(cholesky)/cholesky | solution.py:21
  180.9 22.3 %cholesky.519 = f32[128,128]{1,0:T(8,128)S(1)} custom-call(f32[128,128]{1,0:T(8,128)S(1)} %convolution_subtract_fusion.18), custom_call_target="Cholesky" | custom-call | tf_op jit(solution)/shard_map/jit(cholesky)/cholesky | solution.py:21
  208.3 11.6 %while.10 = (s32[]{:T(128)}, f32[512,512]{1,0:T(8,128)}, s32[4,2]{0,1:T(2,128)S(1)}, f32[4,128,128]{2,1,0:T(8,128)S(1)}, s32[]{:T(128)}) while((s32[]{:T(128)}, f32[512,512]{1,0:T(8,128)}, s32[4,2]{0,1:T(2,128)S(1)}, f32[4,128,128]{2,1,0:T(8,128)S(1)}, s32[]{:T(128)}) %tuple.170), condition=%wide.while_cond, body=%wide.while_body.sunk | while | flops 2 | bytes 131181 | solution.py:22
  219.9 39.3 %custom-call.48 = f32[4,128,128]{1,2,0:T(8,128)S(1)} custom-call(f32[4,128,128]{2,1,0:T(8,128)S(1)} %get-tuple-element.41), custom_call_target="InvertDiagBlocksLowerTriangular" | custom-call | tf_op jit(solution)/shard_map/jit(_solve_triangular)/triangular_solve | solution.py:22
  273.0 11.7 %cholesky.534 = f32[128,128]{1,0:T(8,128)S(1)} custom-call(f32[128,128]{1,0:T(8,128)S(1)} %cholesky.759), custom_call_target="Cholesky" | custom-call | tf_op jit(solution)/shard_map/jit(cholesky)/cholesky | solution.py:24
  284.8 9.8 custom-call.49
  297.9 11.7 %cholesky.553 = f32[128,128]{1,0:T(8,128)S(1)} custom-call(f32[128,128]{1,0:T(8,128)S(1)} %cholesky.763), custom_call_target="Cholesky" | custom-call | tf_op jit(solution)/shard_map/jit(cholesky)/cholesky | solution.py:24
  310.9 9.8 custom-call.50
  322.3 11.7 %cholesky.574 = f32[128,128]{1,0:T(8,128)S(1)} custom-call(f32[128,128]{1,0:T(8,128)S(1)} %cholesky.768), custom_call_target="Cholesky" | custom-call | tf_op jit(solution)/shard_map/jit(cholesky)/cholesky | solution.py:24
  334.8 10.2 %custom-call.51 = f32[1,128,128]{1,2,0:T(8,128)S(1)} custom-call(f32[1,128,128]{2,1,0:T(8,128)S(1)} %get-tuple-element.120), custom_call_target="InvertDiagBlocksLowerTriangular" | custom-call | tf_op jit(solution)/shard_map/jit(cholesky)/cholesky | solution.py:24
  346.4 11.7 %cholesky.591 = f32[128,128]{1,0:T(8,128)S(1)} custom-call(f32[128,128]{1,0:T(8,128)S(1)} %convolution_subtract_fusion.17), custom_call_target="Cholesky" | custom-call | tf_op jit(solution)/shard_map/jit(cholesky)/cholesky | solution.py:24
  361.7 4.4 convolution_bitcast_fusion
  366.2 6.8 collective-permute-start.1
  375.3 22.9 %all-reduce.5 = (f32[1024]{0:T(1024)S(1)}, f32[1024]{0:T(1024)S(1)}) all-reduce(f32[1024]{0:T(1024)S(1)} %dynamic-update-slice.22, f32[1024]{0:T(1024)S(1)} %bitcast_dynamic-update-slice_fusion.4), channel_id=1, replica_groups=mesh['tm'=32,'panel'=16] {'panel'}, use_global_device_ids=true, to_apply=%add.3 | all-reduce | flops 2048 | bytes 16384
  401.6 27.4 %while.12 = (s32[]{:T(128)}, f32[1024,1024]{1,0:T(8,128)}, s32[8,2]{0,1:T(2,128)S(1)}, f32[8,128,128]{2,1,0:T(8,128)}, s32[]{:T(128)}) while((s32[]{:T(128)}, f32[1024,1024]{1,0:T(8,128)}, s32[8,2]{0,1:T(2,128)S(1)}, f32[8,128,128]{2,1,0:T(8,128)}, s32[]{:T(128)}) %tuple.179), condition=%wide.while_cond.1, body=%wide.while_body.1.sunk | while | flops 2 | bytes 132705 | solution.py:66
  429.0 80.0 %custom-call.59 = f32[8,128,128]{1,2,0:T(8,128)} custom-call(f32[8,128,128]{2,1,0:T(8,128)} %get-tuple-element.43), custom_call_target="InvertDiagBlocksLowerTriangular" | custom-call | tf_op jit(solution)/shard_map/jit(_solve_triangular)/triangular_solve/custom-call.2 | solution.py:66
  528.0 3.1 fusion.73
  531.1 16.0 %convert_add_fusion = f32[1024,1024]{0,1:T(8,128)S(1)} fusion(f32[1024,1024]{1,0:T(8,128)} %all-gather.7.cloned.1.call-done, f32[512,512]{1,0:T(8,128)S(1)} %get-tuple-element.84, f32[512,512]{1,0:T(8,128)S(1)} %fusion.28, f32[512,512]{1,0:T(8,128)S(1)} %copy-done.4), kind=kOutput, calls=%fused_computation.8 | convolution fusion | flops 12892241920 | bytes 11534336 | tf_op jit(solution)/shard_map/dot_general | solution.py:54
  551.0 11.7 %cholesky.606 = f32[128,128]{1,0:T(8,128)S(1)} custom-call(f32[128,128]{1,0:T(8,128)S(1)} %cholesky.772), custom_call_target="Cholesky" | custom-call | tf_op jit(solution)/shard_map/jit(cholesky)/cholesky | solution.py:21
  562.9 9.8 custom-call.52
  574.1 11.7 %cholesky.625 = f32[128,128]{1,0:T(8,128)S(1)} custom-call(f32[128,128]{1,0:T(8,128)S(1)} %cholesky.776), custom_call_target="Cholesky" | custom-call | tf_op jit(solution)/shard_map/jit(cholesky)/cholesky | solution.py:21
  587.2 9.9 custom-call.53
  598.7 11.7 %cholesky.646 = f32[128,128]{1,0:T(8,128)S(1)} custom-call(f32[128,128]{1,0:T(8,128)S(1)} %cholesky.781), custom_call_target="Cholesky" | custom-call | tf_op jit(solution)/shard_map/jit(cholesky)/cholesky | solution.py:21
  611.1 9.8 custom-call.54
  621.5 12.1 %cholesky.663 = f32[128,128]{1,0:T(8,128)S(1)} custom-call(f32[128,128]{1,0:T(8,128)S(1)} %convolution_subtract_fusion.16), custom_call_target="Cholesky" | custom-call | tf_op jit(solution)/shard_map/jit(cholesky)/cholesky | solution.py:21
  638.1 11.7 %while.11 = (s32[]{:T(128)}, f32[512,512]{1,0:T(8,128)}, s32[4,2]{0,1:T(2,128)S(1)}, f32[4,128,128]{2,1,0:T(8,128)S(1)}, s32[]{:T(128)}) while((s32[]{:T(128)}, f32[512,512]{1,0:T(8,128)}, s32[4,2]{0,1:T(2,128)S(1)}, f32[4,128,128]{2,1,0:T(8,128)S(1)}, s32[]{:T(128)}) %tuple.188), condition=%wide.while_cond.clone, body=%wide.while_body.clone.sunk | while | flops 2 | bytes 131181 | solution.py:22
  649.8 39.3 %custom-call.55 = f32[4,128,128]{1,2,0:T(8,128)S(1)} custom-call(f32[4,128,128]{2,1,0:T(8,128)S(1)} %get-tuple-element.42), custom_call_target="InvertDiagBlocksLowerTriangular" | custom-call | tf_op jit(solution)/shard_map/jit(_solve_triangular)/triangular_solve | solution.py:22
  696.5 3.6 convolution_subtract_fusion
  703.9 11.7 %cholesky.678 = f32[128,128]{1,0:T(8,128)S(1)} custom-call(f32[128,128]{1,0:T(8,128)S(1)} %cholesky.785), custom_call_target="Cholesky" | custom-call | tf_op jit(solution)/shard_map/jit(cholesky)/cholesky | solution.py:24
  715.7 9.8 custom-call.56
  729.9 11.7 %cholesky.697 = f32[128,128]{1,0:T(8,128)S(1)} custom-call(f32[128,128]{1,0:T(8,128)S(1)} %cholesky.789), custom_call_target="Cholesky" | custom-call | tf_op jit(solution)/shard_map/jit(cholesky)/cholesky | solution.py:24
  743.9 9.8 custom-call.57
  756.2 11.7 %cholesky.718 = f32[128,128]{1,0:T(8,128)S(1)} custom-call(f32[128,128]{1,0:T(8,128)S(1)} %cholesky.794), custom_call_target="Cholesky" | custom-call | tf_op jit(solution)/shard_map/jit(cholesky)/cholesky | solution.py:24
  768.7 10.0 custom-call.58
  780.1 11.7 %cholesky.735 = f32[128,128]{1,0:T(8,128)S(1)} custom-call(f32[128,128]{1,0:T(8,128)S(1)} %convolution_subtract_fusion.15), custom_call_target="Cholesky" | custom-call | tf_op jit(solution)/shard_map/jit(cholesky)/cholesky | solution.py:24
  797.6 22.8 %while.9 = (s32[]{:T(128)}, f32[1024,1024]{1,0:T(8,128)}, s32[8,2]{0,1:T(2,128)S(1)}, f32[8,128,128]{2,1,0:T(8,128)S(1)}, s32[]{:T(128)}) while((s32[]{:T(128)}, f32[1024,1024]{1,0:T(8,128)}, s32[8,2]{0,1:T(2,128)S(1)}, f32[8,128,128]{2,1,0:T(8,128)S(1)}, s32[]{:T(128)}) %tuple.189), condition=%wide.while_cond.2, body=%wide.while_body.2.sunk | while | flops 2 | bytes 131181 | solution.py:57
  820.5 78.8 %custom-call.33 = f32[8,128,128]{1,2,0:T(8,128)S(1)} custom-call(f32[8,128,128]{2,1,0:T(8,128)S(1)} %get-tuple-element.28), custom_call_target="InvertDiagBlocksLowerTriangular" | custom-call | tf_op jit(solution)/shard_map/jit(_solve_triangular)/triangular_solve | solution.py:57
  933.1 64.7 %all-gather.9.cloned.1.call-done = f32[1024,1024]{1,0:T(8,128)} async-done(((f32[64,1024]{1,0:T(8,128)}), f32[1024,1024]{1,0:T(8,128)}) %all-gather.9.cloned.1.call-update) | async-done | bytes 4194320 | tf_op jit(solution)/shard_map/all_gather | solution.py:61
  997.8 7.0 fusion.3
  (341 shorter events, 206.9 us)
Async XLA Ops:
  7.2 354.5 %copy-start = (f32[1,64,1024]{2,1,0:T(8,128)S(1)}, f32[1,64,1024]{2,1,0:T(8,128)}, u32[]{:S(2)}) copy-start(f32[1,64,1024]{2,1,0:T(8,128)} %param.12) | copy-start | bytes 786436
  7.2 87.9 %all-gather.5.cloned.1.call-start = ((), (), s32[]{:S(2)}) async-start(), calls=%async_computation | async-start | bytes 4456448 | tf_op jit(solution)/shard_map/all_gather | solution.py:44
  7.2 9.2 collective-permute-start
  16.5 0.7 copy-start.20
  17.2 514.0 %all-gather.7.cloned.1.call-start = ((), (), s32[]{:S(2)}) async-start(), calls=%async_computation.1 | async-start | bytes 4456448 | tf_op jit(solution)/shard_map/all_gather | solution.py:51
  100.9 1.9 copy-start.2
  127.5 131.7 %copy-start.5 = (f32[512,512]{1,0:T(8,128)S(1)}, f32[512,512]{1,0:T(8,128)}, u32[]{:S(2)}) copy-start(f32[512,512]{1,0:T(8,128)} %get-tuple-element.95) | copy-start | bytes 3145732
  128.2 0.7 copy-start.16
  259.2 1.7 copy-start.18
  272.0 1.0 copy-start.6
  361.7 4.5 copy-start.21
  361.7 13.2 %copy-start.23 = (f32[1,64]{1,0:T(1,128)S(1)}, f32[1,64]{1,0:T(1,128)}, u32[]{:S(2)}) copy-start(f32[1,64]{1,0:T(1,128)} %param.14) | copy-start | bytes 772
  361.7 36.5 %copy-start.4 = (f32[512,512]{1,0:T(8,128)S(1)}, f32[512,512]{1,0:T(8,128)}, u32[]{:S(2)}) copy-start(f32[512,512]{1,0:T(8,128)} %fusion.43) | copy-start | bytes 3145732
  366.1 631.7 %all-gather.9.cloned.1.call-start = ((), (), s32[]{:S(2)}) async-start(), calls=%async_computation.2 | async-start | bytes 4456448 | tf_op jit(solution)/shard_map/all_gather | solution.py:61
  366.2 8.9 collective-permute-start.1
  523.7 4.4 copy-start.22
  547.1 1.9 copy-start.3
  573.4 0.7 copy-start.15
  689.1 3.4 copy-start.19
  694.7 1.8 copy-start.8
  694.8 1.6 copy-start.9
  694.9 1.5 copy-start.10
  702.9 1.0 copy-start.7
  729.2 0.7 copy-start.14
  795.1 108.1 %copy-start.13 = (f32[1024,64]{0,1:T(8,128)S(1)}, f32[1024,64]{0,1:T(8,128)}, u32[]{:S(2)}) copy-start(f32[1024,64]{0,1:T(8,128)} %fusion.73) | copy-start | bytes 786436
  907.5 90.3 %copy-start.17 = (f32[1,64,1024]{2,1,0:T(8,128)S(1)}, f32[1,64,1024]{2,1,0:T(8,128)}, u32[]{:S(2)}) copy-start(f32[1,64,1024]{2,1,0:T(8,128)} %param.11) | copy-start | bytes 786436
  914.5 0.7 copy-start.11
  915.2 82.6 %copy-start.12 = (f32[1024,64]{0,1:T(8,128)S(1)}, f32[1024,64]{0,1:T(8,128)}, u32[]{:S(2)}) copy-start(f32[1024,64]{0,1:T(8,128)} %copy-done.11) | copy-start | bytes 786436
  918.4 86.4 %copy-start.1 = (f32[1,64,1024]{2,1,0:T(8,128)S(1)}, f32[1,64,1024]{2,1,0:T(8,128)}, u32[]{:S(2)}) copy-start(f32[1,64,1024]{2,1,0:T(8,128)} %param.12) | copy-start | bytes 786436
Sparse Core Ops, SparseCore 0:
  17.3 77.7 all-gather.4
  366.2 78.5 all-gather.6
  915.3 82.4 all-gather.8
where the time goes:
time: 1030 us; the launch traced here: 1010 us
  other arithmetic  583 us (57%)
  waiting for transfers between devices  146 us (14%)
  matrix products  122 us (12%)
  local copies, waits for them, and re-layouts  98 us (10%)
  between operations  26.2 us (3%)
  blocking collectives  22.9 us (2%)
  starting transfers between devices  12.5 us (1%)
    another operation x29, other arithmetic, block_cholesky(): first_factor = jnp.linalg.cholesky(top_left)  173 us
    another operation x30, other arithmetic, block_cholesky(): second_factor = jnp.linalg.cholesky(schur_block)  159 us
    another operation x2, other arithmetic, body(): jax.scipy.linalg.solve_triangular(lower_factor, whole_mean, lower=True)  82.5 us
    another operation x3, other arithmetic, body(): jax.scipy.linalg.solve_triangular(inner_factor, mixed_rows.T, lower=True)  81.3 us
    another operation x5, other arithmetic, block_cholesky(): jax.scipy.linalg.solve_triangular(first_factor, bottom_left.T, lower=True)  81.2 us
    all_gather x1, waiting for transfers between devices, body(): lax.all_gather(prev_cov, 'panel', axis=0, tiled=True)  77.9 us
    all_gather x1, waiting for transfers between devices, body(): lax.all_gather(factor_part, 'panel', axis=0, tiled=True)  64.7 us
    another operation x24, local copies, waits for them, and re-layouts, body(): jax.scipy.linalg.solve_triangular(lower_factor, whole_mean, lower=True)  27.3 us
  transfers between devices with their start and end apart: 5, of which 3 were waited for; matrix products, arithmetic and copies ran while one was open for 15% of the time, Pallas kernels for 0%

commit v1 on v0

v1 whole, which is shorter than its diff:
```python
import functools

import jax
import jax.numpy as jnp
from jax import lax
from jax.experimental import pallas as pl
from jax.experimental.pallas import tpu as pltpu
from jax.sharding import PartitionSpec as P

MESH = pl.DeviceIdType.MESH
HIGHEST = lax.Precision.HIGHEST
F32 = jnp.float32
BF16 = jnp.bfloat16
ROWS = 64
HALF = 32
LANES = 128
LAG = 3
TOLERANCE = 1e-5


def split(value):
    high = value.astype(BF16)
    return high, (value - high.astype(F32)).astype(BF16)


def dot(left, right):
    return jnp.dot(left, right, preferred_element_type=F32)


def dot_nt(left, right):
    return lax.dot_general(left, right, (((1,), (1,)), ((), ())), preferred_element_type=F32)


def place(T):
    t = lax.axis_index("tm")
    z = lax.axis_index("panel")
    distance = T // 2
    core = lax.rem(t, 2)
    low = t < distance
    base_low = lax.rem(t, distance) - core
    base_high = base_low + distance
    return t, z, core, low, base_low, base_high


def await_bytes(ref, sem):
    pltpu.make_async_copy(ref, ref, sem).wait()


def solve_kernel(
    T, Z,
    trans, cov, info, mean, infovec,
    rows_out, small_out, pj_out, a_out, v_out,
    pj, av, vv, st_pj, st_v, p_high, p_low, j_high, j_low, series, scale,
    recv, send, shift_recv, shift_send, out_sem,
):
    t, z, core, low, base_low, base_high = place(T)
    supers = Z // 2
    near = supers // 2
    H = Z // 2
    size = Z * ROWS
    partner = t + 1 - 2 * core
    opposite = jnp.where(low, base_high, base_low)
    up, down = lax.rem(z + 1, Z), lax.rem(z + Z - 1, Z)

    barrier = pltpu.get_barrier_semaphore()
    for device in ((t, up), (t, down), (partner, z), (opposite, z), (opposite + 1, z)):
        pl.semaphore_signal(barrier, inc=1, device_id=device, device_id_type=MESH)

    own_super = z // 2
    for k in range(near + 1):
        column = pl.multiple_of(lax.rem(own_super + k, supers) * LANES, LANES)
        block = jnp.where(low, cov[:, pl.ds(column, LANES)], info[:, pl.ds(column, LANES)])
        st_pj[0, k] = block[:HALF]
        st_pj[1, k] = block[HALF:]
    vector = jnp.where(low, mean[...], infovec[...])
    nothing = jnp.zeros_like(vector)
    vector = jnp.where(
        lax.rem(z, 2) == 0,
        jnp.concatenate([vector, nothing], axis=1),
        jnp.concatenate([nothing, vector], axis=1),
    )
    lane = lax.broadcasted_iota(jnp.int32, (8, LANES), 1)
    for h in range(2):
        start = lax.rem(z, 2) * ROWS + h * HALF
        mine = jnp.logical_and(lane >= start, lane < start + HALF)
        st_v[h] = jnp.where(mine, jnp.broadcast_to(vector, (8, LANES)), 0.0)
    pl.semaphore_wait(barrier, 5)

    target_base = jnp.where(core == 0, base_low, base_high)
    high = jnp.logical_not(low)
    low_has_far = own_super < near
    moves = []
    for h in range(2):
        moves += [
            (st_pj.at[h, pl.ds(0, near)], pj.at[h, z, pl.ds(0, near)], 0, h, low),
            (st_pj.at[h, pl.ds(0, near)], pj.at[h, z, pl.ds(near, near)], 1, h, high),
            (st_pj.at[h, near], pj.at[h, z, 2 * near], 2, h, low == low_has_far),
            (st_v.at[h], vv.at[h, z, pl.ds(0, 8)], 3, h, low),
            (st_v.at[h], vv.at[h, z, pl.ds(8, 8)], 4, h, high),
            (trans.at[pl.ds(h * HALF, HALF)], av.at[h, z], 5, h, high),
        ]

    def shift(source, target, k, h):
        return pltpu.make_async_remote_copy(
            src_ref=source, dst_ref=target, send_sem=shift_send.at[k, h], recv_sem=shift_recv.at[k],
            device_id=(target_base + h, z), device_id_type=MESH,
        )

    for source, target, k, h, active in moves:
        here = target_base + h == t

        @pl.when(jnp.logical_and(active, here))
        def _():
            pltpu.make_async_copy(source, target, shift_recv.at[k]).start()

        @pl.when(jnp.logical_and(active, jnp.logical_not(here)))
        def _():
            shift(source, target, k, h).start()

    await_bytes(pj.at[core, z, pl.ds(0, near)], shift_recv.at[0])
    await_bytes(pj.at[core, z, pl.ds(near, near)], shift_recv.at[1])
    await_bytes(pj.at[core, z, 2 * near], shift_recv.at[2])
    await_bytes(vv.at[core, z, pl.ds(0, 8)], shift_recv.at[3])
    await_bytes(vv.at[core, z, pl.ds(8, 8)], shift_recv.at[4])

    def part(kind, h, owner):
        if kind == 0:
            return pj.at[h, owner, pl.ds(0, near)]
        if kind == 1:
            return pj.at[h, owner, pl.ds(near, near + 1)]
        if kind == 2:
            return vv.at[h, owner]
        return av.at[h, owner, pl.ds((kind - 3) * (HALF // 2), HALF // 2)]

    def parts(kind, h, count):
        if kind == 0:
            return pj.at[h, pl.ds(0, count), pl.ds(0, near)]
        if kind == 1:
            return pj.at[h, pl.ds(0, count), pl.ds(near, near + 1)]
        if kind == 2:
            return vv.at[h, pl.ds(0, count)]
        return av.at[h, pl.ds(0, count), pl.ds((kind - 3) * (HALF // 2), HALF // 2)]

    def copy(kind, owner, way):
        device = ((t, up), (t, down), (partner, z))[way]
        ref = part(kind, core, owner)
        return pltpu.make_async_remote_copy(
            src_ref=ref, dst_ref=ref, send_sem=send.at[kind, way], recv_sem=recv.at[kind, core, owner],
            device_id=device, device_id_type=MESH,
        )

    def arrived(kind, h, owner):
        await_bytes(part(kind, h, owner), recv.at[kind, h, owner])

    def begin(kinds):
        for kind in kinds:
            for way in range(3):
                copy(kind, z, way).start()

    def hop(kinds, step):
        before, after = lax.rem(z - step + Z, Z), lax.rem(z + step, Z)
        for kind in kinds:
            arrived(kind, core, before)

            @pl.when(jnp.logical_or(step < H - 1, core == 0))
            def _():
                copy(kind, before, 0).start()

            copy(kind, before, 2).start()
            arrived(kind, core, after)

            @pl.when(jnp.logical_or(step < H - 1, core == 1))
            def _():
                copy(kind, after, 1).start()

            copy(kind, after, 2).start()

    def last_hop(kinds):
        far = lax.rem(z + H, Z)
        for kind in kinds:
            arrived(kind, core, far)
            copy(kind, far, 2).start()

    def completed(step):
        owner = jnp.where(lax.rem(step + z, 2) == 1, lax.rem(z + step, Z), lax.rem(z - step + Z, Z))
        return owner // 2

    def store(index, row, column, block):
        top, rest = split(block)
        where = (pl.ds(pl.multiple_of(row * LANES, LANES), LANES), pl.ds(pl.multiple_of(column * LANES, LANES), LANES))
        (p_high, j_high)[index][where] = top
        (p_low, j_low)[index][where] = rest

    def unpack(step):
        row = completed(step)
        for owner in (2 * row, 2 * row + 1):
            for kind in (0, 1, 2):
                arrived(kind, 1 - core, owner)

        def block(k):
            return jnp.concatenate(
                [pj[0, 2 * row, k], pj[1, 2 * row, k], pj[0, 2 * row + 1, k], pj[1, 2 * row + 1, k]], axis=0
            )

        for index in range(2):
            for k in range(near):
                column = lax.rem(row + k, supers)
                value = block(index * near + k)
                store(index, row, column, value)
                if k:
                    store(index, column, row, value.T)
        column = lax.rem(row + near, supers)
        value = block(2 * near)
        for index in range(2):
            @pl.when((row < near) == (index == 0))
            def _():
                store(index, row, column, value)
                store(index, column, row, value.T)

    matrices = (0, 1, 2)
    states = (3, 4)
    lag = min(LAG, H - 1)
    begin(matrices)

    def first_steps(step, _):
        hop(matrices, step)

        @pl.when(step > 1)
        def _():
            unpack(step - 1)

        return 0

    lax.fori_loop(1, lag + 1, first_steps, 0)
    await_bytes(av.at[core, z], shift_recv.at[5])
    begin(states)

    def later_steps(step, _):
        hop(matrices, step)
        hop(states, step - lag)
        unpack(step - 1)
        return 0

    lax.fori_loop(lag + 1, H, later_steps, 0)
    last_hop(matrices)
    pending = list(range(H - lag, H))

    def next_hop():
        if pending:
            hop(states, pending.pop(0))

    next_hop()
    unpack(H - 1)
    unpack(H)
    pj_save = pltpu.make_async_copy(pj, pj_out, out_sem.at[0])
    v_save = pltpu.make_async_copy(vv, v_out, out_sem.at[1])
    pj_save.start()
    v_save.start()

    width = min(256, size)
    unit = (
        lax.broadcasted_iota(jnp.int32, (width, width), 0) == lax.broadcasted_iota(jnp.int32, (width, width), 1)
    ).astype(F32)
    for q in range(size // width):
        columns = slice(q * width, (q + 1) * width)
        product = dot(p_high[...], j_high[:, columns])
        corner = product[columns]
        inverse = 1.0 / (1.0 + jnp.sum(corner * unit, axis=0, keepdims=True))
        scale[:, columns] = jnp.broadcast_to(inverse, (8, width))
        series[:, columns] = (-product * inverse).astype(BF16)
        series[columns, columns] = (unit - (unit + corner) * inverse).astype(BF16)
    next_hop()

    inverse = scale[0:1]

    def approximate(value):
        first = value * inverse
        result = first
        for _ in range(3):
            result = first + dot(result.astype(BF16), series[...])
        return result

    def exact(value, top, rest):
        count = value.shape[0]
        big, small = split(value)
        both = dot(jnp.concatenate([big, small], axis=0), top[...])
        return both[:count] + both[count:] + dot(big, rest[...])

    def vector_row(k):
        tiles = []
        for s in range(supers):
            tiles.append(
                (vv[0, 2 * s, pl.ds(8 * k, 8)] + vv[1, 2 * s, pl.ds(8 * k, 8)])
                + (vv[0, 2 * s + 1, pl.ds(8 * k, 8)] + vv[1, 2 * s + 1, pl.ds(8 * k, 8)])
            )
        return jnp.concatenate(tiles, axis=1)

    target = av[core, z]
    x = approximate(target)
    stacked = exact(jnp.concatenate([x, vector_row(1)], axis=0), p_high, p_low)
    y = stacked[:HALF]
    combined = vector_row(0) + stacked[HALF:]
    next_hop()
    residual = target - x - exact(y, j_high, j_low)
    change = approximate(residual)
    x = x + change
    moved = exact(change, p_high, p_low)
    y = y + moved
    residual = residual - change - exact(moved, j_high, j_low)
    while pending:
        next_hop()
    last_hop(states)
    change = approximate(residual)
    x = x + change
    moved = dot(change.astype(BF16), p_high[...])
    y = y + moved
    residual = residual - change - dot(moved.astype(BF16), j_high[...])
    error = jnp.sum(residual * residual)
    norm = jnp.sum(target * target)
    good = jnp.where(error <= (TOLERANCE * TOLERANCE) * norm, 1.0, 0.0).astype(F32)
    small_out[0:8] = jnp.zeros((8, LANES), F32)
    small_out[0:8, 0:HALF] = lax.dot_general(
        combined, x, (((1,), (1,)), ((), ())), precision=HIGHEST, preferred_element_type=F32
    )
    small_out[8:16] = jnp.broadcast_to(good, (8, LANES))

    y_high, y_low = split(y)
    y_both = jnp.concatenate([y_high, y_low], axis=0)

    def product_steps(step, _):
        row = completed(step)
        for owner in (2 * row, 2 * row + 1):
            for kind in states:
                arrived(kind, 1 - core, owner)
        block = jnp.concatenate(
            [av[0, 2 * row], av[1, 2 * row], av[0, 2 * row + 1], av[1, 2 * row + 1]], axis=0
        )
        top, rest = split(block)
        both = dot_nt(y_both, top)
        rows_out[:, pl.ds(pl.multiple_of(row * LANES, LANES), LANES)] = (
            both[:HALF] + both[HALF:] + dot_nt(y_high, rest)
        )
        return 0

    lax.fori_loop(1, H + 1, product_steps, 0)
    a_save = pltpu.make_async_copy(av, a_out, out_sem.at[2])
    a_save.start()

    for kind in matrices + states:
        await_bytes(parts(kind, core, Z), send.at[kind, 2])
        for way in range(2):
            @pl.when(core == way)
            def _():
                await_bytes(parts(kind, core, H), send.at[kind, way])

            @pl.when(core != way)
            def _():
                await_bytes(parts(kind, core, H - 1), send.at[kind, way])
    for source, target, k, h, active in moves:
        @pl.when(jnp.logical_and(active, target_base + h != t))
        def _():
            shift(source, target, k, h).wait_send()
    pj_save.wait()
    v_save.wait()
    a_save.wait()


def return_kernel(T, rows, small, cov, mean, cov_out, mean_out, rows_in, small_in, recv, send):
    t, z, core, low, base_low, base_high = place(T)
    high = jnp.logical_not(low)
    owner = jnp.where(low, base_high, base_high + 1)
    partner = t + 1 - 2 * core
    opposite = jnp.where(low, base_high, base_low)
    barrier = pltpu.get_barrier_semaphore()
    for device in ((partner, z), (opposite, z), (opposite + 1, z)):
        pl.semaphore_signal(barrier, inc=1, device_id=device, device_id_type=MESH)
    pl.semaphore_wait(barrier, 3)
    moves = ((rows, rows_in.at[core], 0), (small.at[pl.ds(0, 8)], small_in.at[core], 1))
    here = owner == t

    def back(source, target, k):
        return pltpu.make_async_remote_copy(
            src_ref=source, dst_ref=target, send_sem=send.at[k], recv_sem=recv.at[k, core],
            device_id=(owner, z), device_id_type=MESH,
        )

    for source, target, k in moves:
        @pl.when(here)
        def _():
            pltpu.make_async_copy(source, target, recv.at[k, core]).start()

        @pl.when(jnp.logical_not(here))
        def _():
            back(source, target, k).start()

    @pl.when(low)
    def _():
        cov_out[...] = cov[...]
        mean_out[...] = mean[...]

    @pl.when(high)
    def _():
        for h in range(2):
            await_bytes(rows_in.at[h], recv.at[0, h])
            cov_out[h * HALF : (h + 1) * HALF] = rows_in[h] + cov[h * HALF : (h + 1) * HALF]
            await_bytes(small_in.at[h], recv.at[1, h])
        mean_out[...] = mean[...] + jnp.concatenate([small_in[0, 0:1, 0:HALF], small_in[1, 0:1, 0:HALF]], axis=1)

    for source, target, k in moves:
        @pl.when(jnp.logical_not(here))
        def _():
            back(source, target, k).wait_send()


def by_factors(operands):
    pj, av, vv = operands
    Z = av.shape[1]
    supers = Z // 2
    near = supers // 2
    size = Z * ROWS
    core = lax.rem(lax.axis_index("tm"), 2)
    z = lax.axis_index("panel")
    packed = pj.transpose(1, 0, 3, 2, 4).reshape(supers, LANES, 2 * near + 1, LANES).transpose(0, 2, 1, 3)

    def whole(index):
        grid = [[None] * supers for _ in range(supers)]
        for row in range(supers):
            for k in range(near + 1):
                if k == near and (row < near) != (index == 0):
                    continue
                block = packed[row, 2 * near if k == near else index * near + k]
                column = (row + k) % supers
                grid[row][column] = block
                if k:
                    grid[column][row] = block.T
        return jnp.concatenate([jnp.concatenate(row, axis=1) for row in grid], axis=0)

    cov, info = whole(0), whole(1)
    rows = av.transpose(1, 0, 2, 3).reshape(size, size)
    tiles = vv[:, :, ::8].sum(axis=0).reshape(supers, 2, 2, LANES).sum(axis=1)
    mean, infovec = tiles[:, 0].reshape(size), tiles[:, 1].reshape(size)
    mm = functools.partial(jnp.dot, precision=HIGHEST)
    lower_factor = jnp.linalg.cholesky(cov)
    inner = jnp.eye(size, dtype=F32) + mm(lower_factor.T, mm(info, lower_factor))
    inner_factor = jnp.linalg.cholesky(inner)
    mixed = mm(rows, lower_factor)
    factor = jax.scipy.linalg.solve_triangular(inner_factor, mixed.T, lower=True).T
    mine = lax.dynamic_slice_in_dim(factor, z * ROWS + core * HALF, HALF, 0)
    mixed_mine = lax.dynamic_slice_in_dim(mixed, z * ROWS + core * HALF, HALF, 0)
    right = jax.scipy.linalg.solve_triangular(lower_factor, mean, lower=True) + mm(infovec, lower_factor)
    weight = jax.scipy.linalg.cho_solve((inner_factor, True), right)
    small = jnp.zeros((16, LANES), F32).at[0:8, 0:HALF].set(mm(mixed_mine, weight)[None])
    return mm(mine, factor.T), small


def solution(mesh):
    T, Z = mesh.shape["tm"], mesh.shape["panel"]
    near = Z // 4
    size = Z * ROWS
    vmem = pl.BlockSpec(memory_space=pltpu.VMEM)
    hbm = pl.BlockSpec(memory_space=pl.ANY)
    dma = pltpu.SemaphoreType.DMA
    pj_shape = (2, Z, 2 * near + 1, HALF, LANES)
    a_shape = (2, Z, HALF, size)
    v_shape = (2, Z, 16, LANES)
    struct = lambda *shape: jax.ShapeDtypeStruct(shape, F32)

    def body(elem_trans, elem_cov, elem_info, elem_mean, elem_infovec):
        rows, small, pj, av, vv = pl.pallas_call(
            functools.partial(solve_kernel, T, Z),
            name="gather_and_solve",
            out_shape=(struct(HALF, size), struct(16, LANES), struct(*pj_shape), struct(*a_shape), struct(*v_shape)),
            in_specs=[vmem] * 5,
            out_specs=(vmem, vmem, hbm, hbm, hbm),
            scratch_shapes=[
                pltpu.VMEM(pj_shape, F32),
                pltpu.VMEM(a_shape, F32),
                pltpu.VMEM(v_shape, F32),
                pltpu.VMEM((2, near + 1, HALF, LANES), F32),
                pltpu.VMEM((2, 8, LANES), F32),
            ]
            + [pltpu.VMEM((size, size), BF16)] * 5
            + [
                pltpu.VMEM((8, size), F32),
                dma((5, 2, Z)),
                dma((5, 3)),
                dma((6,)),
                dma((6, 2)),
                dma((3,)),
            ],
            compiler_params=pltpu.CompilerParams(
                collective_id=0, has_side_effects=True, vmem_limit_bytes=48 * 2**20
            ),
        )(elem_trans[0], elem_cov[0], elem_info[0], elem_mean, elem_infovec)
        rows, small = lax.cond(
            small[8, 0] > 0.5, lambda operands: (rows, small), by_factors, (pj, av, vv)
        )
        new_cov, new_mean = pl.pallas_call(
            functools.partial(return_kernel, T),
            name="rows_to_owner",
            out_shape=(struct(ROWS, size), struct(1, ROWS)),
            in_specs=[vmem] * 4,
            out_specs=(vmem, vmem),
            scratch_shapes=[
                pltpu.VMEM((2, HALF, size), F32),
                pltpu.VMEM((2, 8, LANES), F32),
                dma((2, 2)),
                dma((2,)),
            ],
            compiler_params=pltpu.CompilerParams(collective_id=1, has_side_effects=True),
        )(rows, small, elem_cov[0], elem_mean)
        return new_cov[None], new_mean

    matrix, line = P("tm", "panel", None), P("tm", "panel")
    return jax.shard_map(
        body,
        mesh=mesh,
        in_specs=(matrix, matrix, matrix, line, line),
        out_specs=(matrix, line),
        check_vma=False,
    )
```

time: 1030 us -> 98.9 us (0.10); the launches traced: 1010 us -> 98.1 us
  other arithmetic: 583 us -> 0 us
  waiting for transfers between devices: 146 us -> 0 us
  matrix products: 122 us -> 0 us
  local copies, waits for them, and re-layouts: 98 us -> 8.21 us
  Pallas kernels: 0 us -> 88.4 us
  between operations: 26.2 us -> 1.32 us
  blocking collectives: 22.9 us -> 0 us
  starting transfers between devices: 12.5 us -> 0 us
    another operation x69 -> x0, other arithmetic: 577 us -> none  [the longest x29 173 us: block_cholesky(): first_factor = jnp.linalg.cholesky(top_left)]
    all_gather x3 -> x0, waiting for transfers between devices: 143 us -> none  [the longest x1 77.9 us: body(): lax.all_gather(prev_cov, 'panel', axis=0, tiled=True)]
    pallas_call x0 -> x2, Pallas kernels: none -> 88.4 us  [the longest x1 79.1 us: body(): pl.pallas_call(functools.partial(solve_kernel, T, Z), name='gather_and_so...]
    another operation x98 -> x0, matrix products: 82.4 us -> none  [the longest x30 20.5 us: body(): weight = jax.scipy.linalg.cho_solve((inner_factor, True), right_side)]
    another operation x106 -> x0, local copies, waits for them, and re-layouts: 77 us -> none  [the longest x24 27.3 us: body(): jax.scipy.linalg.solve_triangular(lower_factor, whole_mean, lower=True)]
    dot_general x8 -> x0, matrix products: 39.7 us -> none  [the longest x1 16 us: body(): jnp.dot(lower_factor.T, coupling, precision=HIGHEST)]
    unnamed x1 -> x0, blocking collectives: 22.9 us -> none
    ppermute x2 -> x0, starting transfers between devices: 12.4 us -> none  [from_behind(): return lax.ppermute(array, axis, pairs)]
  transfers between devices with their start and end apart: 5 -> 0, of which waited for: 3 -> 0; matrix products, arithmetic and copies ran while one was open for 15% -> 0% of each run, Pallas kernels for 0% -> 0%
where the time goes in v1:
time: 98.9 us; the launch traced here: 98.1 us
  Pallas kernels  88.4 us (89%)
  local copies, waits for them, and re-layouts  8.21 us (8%)
  between operations  1.32 us (1%)
    pallas_call x1, Pallas kernels, body(): pl.pallas_call(functools.partial(solve_kernel, T, Z), name='gather_and_so...  79.1 us
    pallas_call x1, Pallas kernels, body(): pl.pallas_call(functools.partial(return_kernel, T), name='rows_to_owner',...  9.31 us
    unnamed x12, local copies, waits for them, and re-layouts  7.01 us

profile of v1, /device:TPU:1, one launch (start us, length us, event | category | flops | bytes accessed | tf_op | source)
XLA Modules:
  0.0 98.1 jit_solution(103544378198126115)
XLA Ops:
  0.6 0.0 copy-start
  0.6 0.9 copy-done
  1.6 0.0 copy-start.1
  1.6 0.9 copy-done.1
  2.5 0.0 copy-start.2
  2.5 0.9 copy-done.2
  3.5 0.0 copy-start.3
  3.5 0.7 copy-done.3
  4.1 0.0 copy-start.4
  4.1 0.7 copy-done.4
  4.8 79.1 %gather_and_solve.1 = (f32[32,1024]{1,0:T(8,128)}, f32[16,128]{1,0:T(8,128)}, f32[2,16,9,32,128]{4,3,2,1,0:T(8,128)}, f32[2,16,32,1024]{3,2,1,0:T(8,128)}, f32[2,16,16,128]{3,2,1,0:T(8,128)S(1)}) custom-call(f32[64,1024]{1,0:T(8,128)S(1)} %bitcast.1003, f32[64,1024]{1,0:T(8,128)S(1)} %bitcast.1002, f32[64,1024]{1,0:T(8,128)S(1)} %bitcast.1004, ...), custom_call_target="tpu_custom_call" | custom-call | tf_op jit(solution)/shard_map/gather_and_solve/pallas_call | solution.py:469
  83.9 1.2 %slice.581 = f32[1,1]{1,0:T(1,128)} slice(f32[16,128]{1,0:T(8,128)} %get-tuple-element.38), slice={[8:9], [0:1]} | slice | bytes 8 | tf_op jit(solution)/shard_map/slice | solution.py:496
  85.7 0.2 conditional.1
  86.0 9.3 %rows_to_owner.1 = (f32[64,1024]{1,0:T(8,128)}, f32[1,64]{1,0:T(1,128)}) custom-call(f32[32,1024]{1,0:T(8,128)} %get-tuple-element.43.rows, f32[16,128]{1,0:T(8,128)} %get-tuple-element.44.small, f32[64,1024]{1,0:T(8,128)} %bitcast.1001, f32[1,64]{1,0:T(1,128)} %mean.3), custom_call_target="tpu_custom_call" | custom-call | tf_op jit(solution)/shard_map/rows_to_owner/pallas_call | solution.py:498
  95.3 1.7 %copy.729 = f32[1,64,1024]{2,1,0:T(8,128)} copy(f32[1,64,1024]{2,1,0:T(8,128)} %bitcast.1079) | data formatting | bytes 524288
  96.9 1.2 %copy.730 = f32[1,64]{1,0:T(1,128)} copy(f32[1,64]{1,0:T(1,128)} %get-tuple-element.414) | data formatting | bytes 512
Async XLA Ops:
  0.6 1.0 copy-start
  1.6 0.9 copy-start.1
  2.5 0.9 copy-start.2
  3.5 0.7 copy-start.3
  4.1 0.7 copy-start.4

commit v2 on v0

--- a/solution.py
+++ b/solution.py
@@ -1,9 +1,458 @@
+import functools
+
 import jax
 import jax.numpy as jnp
 from jax import lax
+from jax.experimental import pallas as pl
+from jax.experimental.pallas import tpu as pltpu
 from jax.sharding import PartitionSpec as P
 
+MESH = pl.DeviceIdType.MESH
 HIGHEST = lax.Precision.HIGHEST
+F32 = jnp.float32
+BF16 = jnp.bfloat16
+ROWS = 64
+HALF = 32
+LANES = 128
+LAG = 2
+CHUNKS = 2
+LIMIT = 0.16
+
+
+def split(value):
+    high = value.astype(BF16)
+    return high, (value - high.astype(F32)).astype(BF16)
+
+
+def dot(left, right):
+    return jnp.dot(left, right, preferred_element_type=F32)
+
+
+def dot_nt(left, right):
+    return lax.dot_general(left, right, (((1,), (1,)), ((), ())), preferred_element_type=F32)
+
+
+def place(T):
+    t = lax.axis_index("tm")
+    z = lax.axis_index("panel")
+    distance = T // 2
+    core = lax.rem(t, 2)
+    low = t < distance
+    base_low = lax.rem(t, distance) - core
+    base_high = base_low + distance
+    return t, z, core, low, base_low, base_high
+
+
+def await_bytes(ref, sem):
+    pltpu.make_async_copy(ref, ref, sem).wait()
+
+
+def solve_kernel(
+    T, Z,
+    trans, cov, info, mean, infovec,
+    cov_out, mean_out, good_out,
+    pj, av, vec, st_v, state_cov, rows_in, small_in, rows, small, good,
+    p_high, p_low, j_high, j_low, series, square, fourth, scale,
+    recv, send, shift_recv, shift_send, local, back_recv, back_send, good_recv, good_send,
+):
+    t, z, core, low, base_low, base_high = place(T)
+    supers = Z // 2
+    near = supers // 2
+    H = Z // 2
+    size = Z * ROWS
+    partner = t + 1 - 2 * core
+    opposite = jnp.where(low, base_high, base_low)
+    up, down = lax.rem(z + 1, Z), lax.rem(z + Z - 1, Z)
+
+    fast = min(4, T // 2)
+    slow = T // 2 // fast
+    chip = t // 2
+    chip_slow, chip_fast = chip // fast, lax.rem(chip, fast)
+    fast_peers = [(chip_slow * fast + lax.rem(chip_fast + k, fast)) * 2 + core for k in range(1, fast)]
+    slow_peers = [(lax.rem(chip_slow + k, slow) * fast + chip_fast) * 2 + core for k in range(1, slow)]
+    devices = [(t, up), (t, down), (partner, z), (opposite, z), (opposite + 1, z)]
+    devices += [(peer, z) for peer in fast_peers + slow_peers]
+    barrier = pltpu.get_barrier_semaphore()
+    for device in devices:
+        pl.semaphore_signal(barrier, inc=1, device_id=device, device_id_type=MESH)
+
+    fetches = [
+        pltpu.make_async_copy(source, target, local.at[k])
+        for k, (source, target) in enumerate(((mean, vec.at[0]), (infovec, vec.at[1]), (cov, state_cov)))
+    ]
+    for fetch in fetches:
+        fetch.start()
+    fetches[0].wait()
+    fetches[1].wait()
+    vector = jnp.where(low, vec[0], vec[1])
+    nothing = jnp.zeros_like(vector)
+    vector = jnp.where(
+        lax.rem(z, 2) == 0,
+        jnp.concatenate([vector, nothing], axis=1),
+        jnp.concatenate([nothing, vector], axis=1),
+    )
+    lane = lax.broadcasted_iota(jnp.int32, (8, LANES), 1)
+    for h in range(2):
+        start = lax.rem(z, 2) * ROWS + h * HALF
+        mine = jnp.logical_and(lane >= start, lane < start + HALF)
+        st_v[h] = jnp.where(mine, jnp.broadcast_to(vector, (8, LANES)), 0.0)
+    own_super = z // 2
+    pl.semaphore_wait(barrier, len(devices))
+
+    target_base = jnp.where(core == 0, base_low, base_high)
+    high = jnp.logical_not(low)
+    low_has_far = own_super < near
+    far = 2 * near * HALF
+    tail = far + HALF
+    moves = []
+    for h in range(2):
+        here_rows = pl.ds(h * HALF, HALF)
+        for k in range(near + 1):
+            column = pl.ds(pl.multiple_of(lax.rem(own_super + k, supers) * LANES, LANES), LANES)
+            if k < near:
+                moves.append((cov.at[here_rows, column], pj.at[h, z, pl.ds(k * HALF, HALF)], 0, h, low))
+                moves.append((info.at[here_rows, column], pj.at[h, z, pl.ds((near + k) * HALF, HALF)], 1, h, high))
+            else:
+                block = pj.at[h, z, pl.ds(far, HALF)]
+                moves.append((cov.at[here_rows, column], block, 2, h, jnp.logical_and(low, low_has_far)))
+                moves.append(
+                    (info.at[here_rows, column], block, 2, h, jnp.logical_and(high, jnp.logical_not(low_has_far)))
+                )
+        moves.append((st_v.at[h], pj.at[h, z, pl.ds(tail, 8)], 3, h, low))
+        moves.append((st_v.at[h], pj.at[h, z, pl.ds(tail + 8, 8)], 4, h, high))
+    state_moves = [(trans.at[pl.ds(h * HALF, HALF)], av.at[h, z], 5, h, high) for h in range(2)]
+
+    def shift(source, target, k, h):
+        return pltpu.make_async_remote_copy(
+            src_ref=source, dst_ref=target, send_sem=shift_send.at[k, h], recv_sem=shift_recv.at[k],
+            device_id=(target_base + h, z), device_id_type=MESH,
+        )
+
+    def start_moves(chosen):
+        for source, target, k, h, active in chosen:
+            here = target_base + h == t
+
+            @pl.when(jnp.logical_and(active, here))
+            def _():
+                pltpu.make_async_copy(source, target, shift_recv.at[k]).start()
+
+            @pl.when(jnp.logical_and(active, jnp.logical_not(here)))
+            def _():
+                shift(source, target, k, h).start()
+
+    start_moves(moves)
+    await_bytes(pj.at[core, z, pl.ds(0, near * HALF)], shift_recv.at[0])
+    await_bytes(pj.at[core, z, pl.ds(near * HALF, near * HALF)], shift_recv.at[1])
+    await_bytes(pj.at[core, z, pl.ds(far, HALF)], shift_recv.at[2])
+    await_bytes(pj.at[core, z, pl.ds(tail, 8)], shift_recv.at[3])
+    await_bytes(pj.at[core, z, pl.ds(tail + 8, 8)], shift_recv.at[4])
+
+    def part(kind, h, owner):
+        buffer, rows_each = ((pj, (tail + 16) // CHUNKS), (av, HALF // CHUNKS))[kind // CHUNKS]
+        return buffer.at[h, owner, pl.ds(kind % CHUNKS * rows_each, rows_each)]
+
+    def parts(kind, h, count):
+        buffer, rows_each = ((pj, (tail + 16) // CHUNKS), (av, HALF // CHUNKS))[kind // CHUNKS]
+        return buffer.at[h, pl.ds(0, count), pl.ds(kind % CHUNKS * rows_each, rows_each)]
+
+    def copy(kind, owner, way):
+        device = ((t, up), (t, down), (partner, z))[way]
+        ref = part(kind, core, owner)
+        return pltpu.make_async_remote_copy(
+            src_ref=ref, dst_ref=ref, send_sem=send.at[kind, way], recv_sem=recv.at[kind, core, owner],
+            device_id=device, device_id_type=MESH,
+        )
+
+    def arrived(kind, h, owner):
+        await_bytes(part(kind, h, owner), recv.at[kind, h, owner])
+
+    def begin(kinds):
+        for kind in kinds:
+            for way in range(3):
+                copy(kind, z, way).start()
+
+    def hop(kinds, step):
+        before, after = lax.rem(z - step + Z, Z), lax.rem(z + step, Z)
+        for kind in kinds:
+            arrived(kind, core, before)
+
+            @pl.when(jnp.logical_or(step < H - 1, core == 0))
+            def _():
+                copy(kind, before, 0).start()
+
+            arrived(kind, core, after)
+
+            @pl.when(jnp.logical_or(step < H - 1, core == 1))
+            def _():
+                copy(kind, after, 1).start()
+
+            copy(kind, before, 2).start()
+            copy(kind, after, 2).start()
+
+    def last_hop(kinds):
+        far = lax.rem(z + H, Z)
+        for kind in kinds:
+            arrived(kind, core, far)
+            copy(kind, far, 2).start()
+
+    def completed(step):
+        owner = jnp.where(lax.rem(step + z, 2) == 1, lax.rem(z + step, Z), lax.rem(z - step + Z, Z))
+        return owner // 2
+
+    def store(index, row, column, block):
+        top, rest = split(block)
+        where = (pl.ds(pl.multiple_of(row * LANES, LANES), LANES), pl.ds(pl.multiple_of(column * LANES, LANES), LANES))
+        (p_high, j_high)[index][where] = top
+        (p_low, j_low)[index][where] = rest
+
+    def unpack(step):
+        row = completed(step)
+        for owner in (2 * row, 2 * row + 1):
+            for kind in matrices:
+                arrived(kind, 1 - core, owner)
+
+        def block(k):
+            return jnp.concatenate(
+                [pj[h, 2 * row + i, k * HALF : (k + 1) * HALF] for i in range(2) for h in range(2)], axis=0
+            )
+
+        for index in range(2):
+            for k in range(near):
+                column = lax.rem(row + k, supers)
+                value = block(index * near + k)
+                store(index, row, column, value)
+                if k:
+                    store(index, column, row, value.T)
+        column = lax.rem(row + near, supers)
+        value = block(2 * near)
+        for index in range(2):
+            @pl.when((row < near) == (index == 0))
+            def _():
+                store(index, row, column, value)
+                store(index, column, row, value.T)
+
+    matrices, states = tuple(range(CHUNKS)), tuple(range(CHUNKS, 2 * CHUNKS))
+    lag = min(LAG, H - 1)
+    begin(matrices)
+    start_moves(state_moves)
+
+    def first_steps(step, _):
+        hop(matrices, step)
+
+        @pl.when(step > 1)
+        def _():
+            unpack(step - 1)
+
+        return 0
+
+    lax.fori_loop(1, lag + 1, first_steps, 0)
+    await_bytes(av.at[core, z], shift_recv.at[5])
+    begin(states)
+
+    def later_steps(step, _):
+        hop(matrices, step)
+        hop(states, step - lag)
+        unpack(step - 1)
+        return 0
+
+    lax.fori_loop(lag + 1, H, later_steps, 0)
+    last_hop(matrices)
+    pending = list(range(H - lag, H))
+
+    def next_hop():
+        if pending:
+            hop(states, pending.pop(0))
+
+    next_hop()
+    unpack(H - 1)
+    unpack(H)
+    width = min(256, size)
+    unit = (
+        lax.broadcasted_iota(jnp.int32, (width, width), 0) == lax.broadcasted_iota(jnp.int32, (width, width), 1)
+    ).astype(F32)
+    for q in range(size // width):
+        columns = slice(q * width, (q + 1) * width)
+        product = dot(p_high[...], j_high[:, columns])
+        corner = product[columns]
+        inverse = 1.0 / (1.0 + jnp.sum(corner * unit, axis=0, keepdims=True))
+        scale[:, columns] = jnp.broadcast_to(inverse, (8, width))
+        series[:, columns] = (-product * inverse).astype(BF16)
+        series[columns, columns] = (unit - (unit + corner) * inverse).astype(BF16)
+    next_hop()
+    total = 0.0
+    for source, target in ((series, square), (square, fourth)):
+        for q in range(size // width):
+            columns = slice(q * width, (q + 1) * width)
+            product = dot(source[...], source[:, columns])
+            target[:, columns] = product.astype(BF16)
+            if target is fourth:
+                total = total + jnp.sum(product * product)
+        next_hop()
+
+    def agree(value, axis, index, peers):
+        good[axis, index] = value
+        copies = [
+            pltpu.make_async_remote_copy(
+                src_ref=good.at[axis, index], dst_ref=good.at[axis, index], send_sem=good_send.at[axis, k],
+                recv_sem=good_recv.at[axis, index], device_id=(peer, z), device_id_type=MESH,
+            )
+            for k, peer in enumerate(peers)
+        ]
+        for one in copies:
+            one.start()
+
+        def result():
+            count = len(peers) + 1
+            for k in range(1, count):
+                other = lax.rem(index + k, count)
+                await_bytes(good.at[axis, other], good_recv.at[axis, other])
+            value = good[axis, 0]
+            for k in range(1, count):
+                value = jnp.minimum(value, good[axis, k])
+            for one in copies:
+                one.wait_send()
+            return value
+
+        return result
+
+    bounded = jnp.where(total <= LIMIT * LIMIT, 1.0, 0.0).astype(F32)
+    fast_result = agree(jnp.broadcast_to(bounded, (8, LANES)), 0, chip_fast, fast_peers)
+
+    inverse = scale[0:1]
+
+    def approximate(value):
+        result = value * inverse
+        for factor in (series, square, fourth):
+            result = result + dot(result.astype(BF16), factor[...])
+        return result
+
+    def exact(value, top, rest):
+        count = value.shape[0]
+        big, small = split(value)
+        both = dot(jnp.concatenate([big, small], axis=0), top[...])
+        return both[:count] + both[count:] + dot(big, rest[...])
+
+    def vector_row(k):
+        at = slice(tail + 8 * k, tail + 8 * k + 8)
+        tiles = [
+            (pj[0, 2 * s, at] + pj[1, 2 * s, at]) + (pj[0, 2 * s + 1, at] + pj[1, 2 * s + 1, at])
+            for s in range(supers)
+        ]
+        return jnp.concatenate(tiles, axis=1)
+
+    target = av[core, z]
+    x = approximate(target)
+    stacked = exact(jnp.concatenate([x, vector_row(1)], axis=0), p_high, p_low)
+    y = stacked[:HALF]
+    combined = vector_row(0) + stacked[HALF:]
+    next_hop()
+    residual = target - x - exact(y, j_high, j_low)
+    change = approximate(residual)
+    x = x + change
+    moved = exact(change, p_high, p_low)
+    y = y + moved
+    residual = residual - change - exact(moved, j_high, j_low)
+    slow_result = agree(fast_result(), 1, chip_slow, slow_peers)
+    while pending:
+        next_hop()
+    last_hop(states)
+    change = approximate(residual)
+    x = x + change
+    moved = dot(change.astype(BF16), p_high[...])
+    y = y + moved
+    small[...] = jnp.zeros((8, LANES), F32)
+    small[:, 0:HALF] = lax.dot_general(
+        combined, x, (((1,), (1,)), ((), ())), precision=HIGHEST, preferred_element_type=F32
+    )
+    owner_device = jnp.where(low, base_high, base_high + 1)
+    mine = owner_device == t
+
+    def give(source, target, arrival, departure):
+        @pl.when(mine)
+        def _():
+            pltpu.make_async_copy(source, target, arrival).start()
+
+        @pl.when(jnp.logical_not(mine))
+        def _():
+            pltpu.make_async_remote_copy(
+                src_ref=source, dst_ref=target, send_sem=departure, recv_sem=arrival,
+                device_id=(owner_device, z), device_id_type=MESH,
+            ).start()
+
+    give(small, small_in.at[core], back_recv.at[supers, core], back_send.at[1])
+
+    y_high, y_low = split(y)
+    y_both = jnp.concatenate([y_high, y_low], axis=0)
+
+    def product_steps(step, _):
+        row = completed(step)
+        for owner in (2 * row, 2 * row + 1):
+            for kind in states:
+                arrived(kind, 1 - core, owner)
+        block = jnp.concatenate(
+            [av[0, 2 * row], av[1, 2 * row], av[0, 2 * row + 1], av[1, 2 * row + 1]], axis=0
+        )
+        top, rest = split(block)
+        both = dot_nt(y_both, top)
+        rows[row] = both[:HALF] + both[HALF:] + dot_nt(y_high, rest)
+        give(rows.at[row], rows_in.at[core, row], back_recv.at[row, core], back_send.at[0])
+        return 0
+
+    lax.fori_loop(1, H + 1, product_steps, 0)
+    good_out[...] = slow_result()
+    fetches[2].wait()
+
+    @pl.when(low)
+    def _():
+        cov_out[...] = state_cov[...]
+        mean_out[...] = vec[0]
+
+    @pl.when(high)
+    def _():
+        for step in range(1, H + 1):
+            row = completed(step)
+            column = pl.ds(pl.multiple_of(row * LANES, LANES), LANES)
+            for h in range(2):
+                await_bytes(rows_in.at[h, row], back_recv.at[row, h])
+                cov_out[h * HALF : (h + 1) * HALF, column] = (
+                    rows_in[h, row] + state_cov[h * HALF : (h + 1) * HALF, column]
+                )
+        for h in range(2):
+            await_bytes(small_in.at[h], back_recv.at[supers, h])
+        mean_out[...] = vec[0] + jnp.concatenate([small_in[0, 0:1, 0:HALF], small_in[1, 0:1, 0:HALF]], axis=1)
+
+    for kind in matrices + states:
+        await_bytes(parts(kind, core, Z), send.at[kind, 2])
+        for way in range(2):
+            @pl.when(core == way)
+            def _():
+                await_bytes(parts(kind, core, H), send.at[kind, way])
+
+            @pl.when(core != way)
+            def _():
+                await_bytes(parts(kind, core, H - 1), send.at[kind, way])
+    for h in range(2):
+        away = target_base + h != t
+        for k, count in ((0, near), (1, near), (2, 1)):
+            side = (low, high, low == low_has_far)[k]
+
+            @pl.when(jnp.logical_and(side, away))
+            def _():
+                await_bytes(pj.at[h, 0, pl.ds(0, count * HALF)], shift_send.at[k, h])
+
+        for k, side in ((3, low), (4, high)):
+            @pl.when(jnp.logical_and(side, away))
+            def _():
+                await_bytes(st_v.at[h], shift_send.at[k, h])
+
+        @pl.when(jnp.logical_and(high, away))
+        def _():
+            await_bytes(av.at[h, 0], shift_send.at[5, h])
+
+    @pl.when(jnp.logical_not(mine))
+    def _():
+        await_bytes(rows, back_send.at[0])
+        await_bytes(small, back_send.at[1])
 
 
 def from_behind(array, axis, by):
@@ -29,7 +478,7 @@
     return jnp.concatenate([upper_rows, lower_rows], axis=0)
 
 
-def body(elem_trans, elem_cov, elem_info, elem_mean, elem_infovec):
+def by_factors(elem_trans, elem_cov, elem_info, elem_mean, elem_infovec):
     distance = lax.axis_size("tm") // 2
     transition = elem_trans[0]
     covariance = elem_cov[0]
@@ -73,16 +522,62 @@
 
 
 def solution(mesh):
+    T, Z = mesh.shape["tm"], mesh.shape["panel"]
+    near = Z // 4
+    size = Z * ROWS
+    vmem = pl.BlockSpec(memory_space=pltpu.VMEM)
+    hbm = pl.BlockSpec(memory_space=pltpu.HBM)
+    dma = pltpu.SemaphoreType.DMA
+    supers = Z // 2
+    struct = lambda *shape: jax.ShapeDtypeStruct(shape, F32)
+    scratch = lambda *shape: pltpu.VMEM(shape, F32)
+
+    def body(*arrays):
+        elem_trans, elem_cov, elem_info, elem_mean, elem_infovec = arrays
+        new_cov, new_mean, good = pl.pallas_call(
+            functools.partial(solve_kernel, T, Z),
+            name="gather_and_solve",
+            out_shape=(struct(ROWS, size), struct(1, ROWS), struct(8, LANES)),
+            in_specs=[hbm] * 5,
+            out_specs=(vmem, vmem, vmem),
+            scratch_shapes=[
+                scratch(2, Z, (2 * near + 1) * HALF + 16, LANES),
+                scratch(2, Z, HALF, size),
+                scratch(2, 1, ROWS),
+                scratch(2, 8, LANES),
+                scratch(ROWS, size),
+                scratch(2, supers, HALF, LANES),
+                scratch(2, 8, LANES),
+                scratch(supers, HALF, LANES),
+                scratch(8, LANES),
+                scratch(2, 4, 8, LANES),
+            ]
+            + [pltpu.VMEM((size, size), BF16)] * 7
+            + [
+                scratch(8, size),
+                dma((2 * CHUNKS, 2, Z)),
+                dma((2 * CHUNKS, 3)),
+                dma((6,)),
+                dma((6, 2)),
+                dma((3,)),
+                dma((supers + 1, 2)),
+                dma((2,)),
+                dma((2, 4)),
+                dma((2, 4)),
+            ],
+            compiler_params=pltpu.CompilerParams(
+                collective_id=0, has_side_effects=True, vmem_limit_bytes=48 * 2**20
+            ),
+        )(elem_trans[0], elem_cov[0], elem_info[0], elem_mean, elem_infovec)
+        return lax.cond(
+            good[0, 0] > 0.5, lambda *_: (new_cov[None], new_mean), by_factors, *arrays
+        )
+
+    matrix, line = P("tm", "panel", None), P("tm", "panel")
     return jax.shard_map(
         body,
         mesh=mesh,
-        in_specs=(
-            P("tm", "panel", None),
-            P("tm", "panel", None),
-            P("tm", "panel", None),
-            P("tm", "panel"),
-            P("tm", "panel"),
-        ),
-        out_specs=(P("tm", "panel", None), P("tm", "panel")),
+        in_specs=(matrix, matrix, matrix, line, line),
+        out_specs=(matrix, line),
         check_vma=False,
     )

time: 1030 us -> 104 us (0.10); the launches traced: 1010 us -> 103 us
  other arithmetic: 583 us -> 0 us
  waiting for transfers between devices: 146 us -> 0 us
  matrix products: 122 us -> 0 us
  local copies, waits for them, and re-layouts: 98 us -> 3.27 us
  Pallas kernels: 0 us -> 85.2 us
  blocking collectives: 22.9 us -> 0 us
  starting transfers between devices: 12.5 us -> 0 us
  between operations: 26.2 us -> 14.7 us
    another operation x69 -> x0, other arithmetic: 577 us -> none  [the longest x29 173 us: block_cholesky(): first_factor = jnp.linalg.cholesky(top_left)]
    all_gather x3 -> x0, waiting for transfers between devices: 143 us -> none  [the longest x1 77.9 us: body(): lax.all_gather(prev_cov, 'panel', axis=0, tiled=True)]
    pallas_call x0 -> x1, Pallas kernels: none -> 85.2 us  [body(): pl.pallas_call(functools.partial(solve_kernel, T, Z), name='gather_and_so...]
    another operation x98 -> x0, matrix products: 82.4 us -> none  [the longest x30 20.5 us: body(): weight = jax.scipy.linalg.cho_solve((inner_factor, True), right_side)]
    another operation x106 -> x0, local copies, waits for them, and re-layouts: 77 us -> none  [the longest x24 27.3 us: body(): jax.scipy.linalg.solve_triangular(lower_factor, whole_mean, lower=True)]
    dot_general x8 -> x0, matrix products: 39.7 us -> none  [the longest x1 16 us: body(): jnp.dot(lower_factor.T, coupling, precision=HIGHEST)]
    unnamed x1 -> x0, blocking collectives: 22.9 us -> none
    ppermute x2 -> x0, starting transfers between devices: 12.4 us -> none  [from_behind(): return lax.ppermute(array, axis, pairs)]
  transfers between devices with their start and end apart: 5 -> 0, of which waited for: 3 -> 0; matrix products, arithmetic and copies ran while one was open for 15% -> 0% of each run, Pallas kernels for 0% -> 0%
where the time goes in v2:
time: 104 us; the launch traced here: 103 us
  Pallas kernels  85.2 us (82%)
  between operations  14.7 us (14%)
  local copies, waits for them, and re-layouts  3.27 us (3%)
    pallas_call x1, Pallas kernels, body(): pl.pallas_call(functools.partial(solve_kernel, T, Z), name='gather_and_so...  85.2 us
    unnamed x2, local copies, waits for them, and re-layouts  2.75 us

profile of v2, /device:TPU:1, one launch (start us, length us, event | category | flops | bytes accessed | tf_op | source)
XLA Modules:
  0.0 103.3 jit_solution(10994925933346722514)
XLA Ops:
  7.2 85.2 %gather_and_solve.1 = (f32[64,1024]{1,0:T(8,128)}, f32[1,64]{1,0:T(1,128)}, f32[8,128]{1,0:T(8,128)S(1)}) custom-call(f32[64,1024]{1,0:T(8,128)} %bitcast.576, f32[64,1024]{1,0:T(8,128)} %bitcast.574, f32[64,1024]{1,0:T(8,128)} %bitcast.577, f32[1,64]{1,0:T(1,128)} %mean.1, f32[1,64]{1,0:T(1,128)} %infovec.1), custom_call_target="tpu_custom_call" | custom-call | tf_op jit(solution)/shard_map/gather_and_solve/pallas_call | solution.py:537
  92.3 0.5 slice.308
  93.5 0.2 conditional.1
  93.7 1.7 %copy.213 = f32[1,64,1024]{2,1,0:T(8,128)} copy(f32[1,64,1024]{2,1,0:T(8,128)} %get-tuple-element.452) | data formatting | bytes 524288
  95.4 1.1 %copy.214 = f32[1,64]{1,0:T(1,128)} copy(f32[1,64]{1,0:T(1,128)} %get-tuple-element.453) | data formatting | bytes 512

commit v3 on v2

--- a/solution.py
+++ b/solution.py
@@ -50,10 +50,10 @@
 def solve_kernel(
     T, Z,
     trans, cov, info, mean, infovec,
-    cov_out, mean_out, good_out,
+    cov_out, mean_out, good_out, pj_out, a_out,
     pj, av, vec, st_v, state_cov, rows_in, small_in, rows, small, good,
     p_high, p_low, j_high, j_low, series, square, fourth, scale,
-    recv, send, shift_recv, shift_send, local, back_recv, back_send, good_recv, good_send,
+    recv, send, shift_recv, shift_send, local, back_recv, back_send, good_recv, good_send, save,
 ):
     t, z, core, low, base_low, base_high = place(T)
     supers = Z // 2
@@ -266,6 +266,9 @@
     next_hop()
     unpack(H - 1)
     unpack(H)
+    pj_save = pltpu.make_async_copy(pj, pj_out, save.at[0])
+    pj_save.start()
+
     width = min(256, size)
     unit = (
         lax.broadcasted_iota(jnp.int32, (width, width), 0) == lax.broadcasted_iota(jnp.int32, (width, width), 1)
@@ -399,6 +402,8 @@
         return 0
 
     lax.fori_loop(1, H + 1, product_steps, 0)
+    a_save = pltpu.make_async_copy(av, a_out, save.at[1])
+    a_save.start()
     good_out[...] = slow_result()
     fetches[2].wait()
 
@@ -431,6 +436,8 @@
             @pl.when(core != way)
             def _():
                 await_bytes(parts(kind, core, H - 1), send.at[kind, way])
+    pj_save.wait()
+    a_save.wait()
     for h in range(2):
         away = target_base + h != t
         for k, count in ((0, near), (1, near), (2, 1)):
@@ -455,70 +462,94 @@
         await_bytes(small, back_send.at[1])
 
 
-def from_behind(array, axis, by):
-    devices = lax.axis_size(axis)
-    pairs = [(i, i + by) for i in range(devices) if 0 <= i + by < devices]
-    return lax.ppermute(array, axis, pairs)
-
-
-def block_cholesky(matrix):
-    state_count = matrix.shape[0]
-    split = state_count // 2
-    top_left = matrix[:split, :split]
-    bottom_left = matrix[split:, :split]
-    bottom_right = matrix[split:, split:]
-    first_factor = jnp.linalg.cholesky(top_left)
-    side_block = jax.scipy.linalg.solve_triangular(first_factor, bottom_left.T, lower=True).T
-    schur_block = bottom_right - jnp.dot(side_block, side_block.T, precision=HIGHEST)
-    second_factor = jnp.linalg.cholesky(schur_block)
-    upper_rows = jnp.concatenate(
-        [first_factor, jnp.zeros((split, state_count - split), jnp.float32)], axis=1
-    )
-    lower_rows = jnp.concatenate([side_block, second_factor], axis=1)
-    return jnp.concatenate([upper_rows, lower_rows], axis=0)
-
-
-def by_factors(elem_trans, elem_cov, elem_info, elem_mean, elem_infovec):
-    distance = lax.axis_size("tm") // 2
-    transition = elem_trans[0]
-    covariance = elem_cov[0]
-    information = elem_info[0]
-    state_mean = elem_mean[0]
-    info_vector = elem_infovec[0]
-    state_count = covariance.shape[1]
-    upper = lax.axis_index("tm") >= distance
-    identity_matrix = jnp.eye(state_count, dtype=jnp.float32)
-    prev_cov, prev_mean = from_behind((covariance, state_mean), "tm", distance)
-    whole_cov, whole_mean = (
-        lax.all_gather(prev_cov, "panel", axis=0, tiled=True),
-        lax.all_gather(prev_mean, "panel", axis=0, tiled=True),
-    )
-    whole_cov = jnp.where(upper, whole_cov, identity_matrix)
-    lower_factor = block_cholesky(whole_cov)
-    coupling_rows = jnp.dot(information, lower_factor, precision=HIGHEST)
-    coupling, whole_vector = (
-        lax.all_gather(coupling_rows, "panel", axis=0, tiled=True),
-        lax.all_gather(info_vector, "panel", axis=0, tiled=True),
-    )
-    inner = identity_matrix + jnp.dot(lower_factor.T, coupling, precision=HIGHEST)
-    inner_factor = block_cholesky(inner)
-    mixed_rows = jnp.dot(transition, lower_factor, precision=HIGHEST)
-    factor_part = jax.scipy.linalg.solve_triangular(inner_factor, mixed_rows.T, lower=True).T
-    combined_rows = (
-        jnp.dot(
-            factor_part,
-            lax.all_gather(factor_part, "panel", axis=0, tiled=True).T,
-            precision=HIGHEST,
+def return_kernel(T, rows, small, cov, mean, cov_out, mean_out, rows_in, small_in, recv, send):
+    t, z, core, low, base_low, base_high = place(T)
+    high = jnp.logical_not(low)
+    owner = jnp.where(low, base_high, base_high + 1)
+    partner = t + 1 - 2 * core
+    opposite = jnp.where(low, base_high, base_low)
+    barrier = pltpu.get_barrier_semaphore()
+    for device in ((partner, z), (opposite, z), (opposite + 1, z)):
+        pl.semaphore_signal(barrier, inc=1, device_id=device, device_id_type=MESH)
+    pl.semaphore_wait(barrier, 3)
+    moves = ((rows, rows_in.at[core], 0), (small, small_in.at[core], 1))
+    here = owner == t
+
+    def back(source, target, k):
+        return pltpu.make_async_remote_copy(
+            src_ref=source, dst_ref=target, send_sem=send.at[k], recv_sem=recv.at[k, core],
+            device_id=(owner, z), device_id_type=MESH,
         )
-        + covariance
-    )
-    right_side = jax.scipy.linalg.solve_triangular(lower_factor, whole_mean, lower=True)
-    right_side = right_side + jnp.dot(whole_vector, lower_factor, precision=HIGHEST)
-    weight = jax.scipy.linalg.cho_solve((inner_factor, True), right_side)
-    combined_mean = jnp.dot(mixed_rows, weight, precision=HIGHEST) + state_mean
-    result_cov = jnp.where(upper, combined_rows, covariance)
-    result_mean = jnp.where(upper, combined_mean, state_mean)
-    return (result_cov[None], result_mean[None])
+
+    for source, target, k in moves:
+        @pl.when(here)
+        def _():
+            pltpu.make_async_copy(source, target, recv.at[k, core]).start()
+
+        @pl.when(jnp.logical_not(here))
+        def _():
+            back(source, target, k).start()
+
+    @pl.when(low)
+    def _():
+        cov_out[...] = cov[...]
+        mean_out[...] = mean[...]
+
+    @pl.when(high)
+    def _():
+        for h in range(2):
+            await_bytes(rows_in.at[h], recv.at[0, h])
+            cov_out[h * HALF : (h + 1) * HALF] = rows_in[h] + cov[h * HALF : (h + 1) * HALF]
+            await_bytes(small_in.at[h], recv.at[1, h])
+        mean_out[...] = mean[...] + jnp.concatenate([small_in[0, 0:1, 0:HALF], small_in[1, 0:1, 0:HALF]], axis=1)
+
+    for source, target, k in moves:
+        @pl.when(jnp.logical_not(here))
+        def _():
+            back(source, target, k).wait_send()
+
+
+def by_factors(operands):
+    pj, av = operands
+    Z = av.shape[1]
+    supers = Z // 2
+    near = supers // 2
+    size = Z * ROWS
+    core = lax.rem(lax.axis_index("tm"), 2)
+    z = lax.axis_index("panel")
+    blocks = 2 * near + 1
+    packed = pj[:, :, : blocks * HALF].reshape(2, supers, 2, blocks, HALF, LANES)
+    packed = packed.transpose(1, 3, 2, 0, 4, 5).reshape(supers, blocks, LANES, LANES)
+
+    def whole(index):
+        grid = [[None] * supers for _ in range(supers)]
+        for row in range(supers):
+            for k in range(near + 1):
+                if k == near and (row < near) != (index == 0):
+                    continue
+                block = packed[row, 2 * near if k == near else index * near + k]
+                column = (row + k) % supers
+                grid[row][column] = block
+                if k:
+                    grid[column][row] = block.T
+        return jnp.concatenate([jnp.concatenate(row, axis=1) for row in grid], axis=0)
+
+    cov, info = whole(0), whole(1)
+    rows = av.transpose(1, 0, 2, 3).reshape(size, size)
+    tiles = pj[:, :, blocks * HALF :: 8].sum(axis=0).reshape(supers, 2, 2, LANES).sum(axis=1)
+    mean, infovec = tiles[:, 0].reshape(size), tiles[:, 1].reshape(size)
+    mm = functools.partial(jnp.dot, precision=HIGHEST)
+    lower_factor = jnp.linalg.cholesky(cov)
+    inner = jnp.eye(size, dtype=F32) + mm(lower_factor.T, mm(info, lower_factor))
+    inner_factor = jnp.linalg.cholesky(inner)
+    mixed = mm(rows, lower_factor)
+    factor = jax.scipy.linalg.solve_triangular(inner_factor, mixed.T, lower=True).T
+    mine = lax.dynamic_slice_in_dim(factor, z * ROWS + core * HALF, HALF, 0)
+    mixed_mine = lax.dynamic_slice_in_dim(mixed, z * ROWS + core * HALF, HALF, 0)
+    right = jax.scipy.linalg.solve_triangular(lower_factor, mean, lower=True) + mm(infovec, lower_factor)
+    weight = jax.scipy.linalg.cho_solve((inner_factor, True), right)
+    small = jnp.zeros((8, LANES), F32).at[:, 0:HALF].set(mm(mixed_mine, weight)[None])
+    return mm(mine, factor.T), small
 
 
 def solution(mesh):
@@ -529,20 +560,24 @@
     hbm = pl.BlockSpec(memory_space=pltpu.HBM)
     dma = pltpu.SemaphoreType.DMA
     supers = Z // 2
+    pj_shape = (2, Z, (2 * near + 1) * HALF + 16, LANES)
+    a_shape = (2, Z, HALF, size)
     struct = lambda *shape: jax.ShapeDtypeStruct(shape, F32)
     scratch = lambda *shape: pltpu.VMEM(shape, F32)
 
     def body(*arrays):
         elem_trans, elem_cov, elem_info, elem_mean, elem_infovec = arrays
-        new_cov, new_mean, good = pl.pallas_call(
+        new_cov, new_mean, good, pj, av = pl.pallas_call(
             functools.partial(solve_kernel, T, Z),
             name="gather_and_solve",
-            out_shape=(struct(ROWS, size), struct(1, ROWS), struct(8, LANES)),
+            out_shape=(
+                struct(ROWS, size), struct(1, ROWS), struct(8, LANES), struct(*pj_shape), struct(*a_shape)
+            ),
             in_specs=[hbm] * 5,
-            out_specs=(vmem, vmem, vmem),
+            out_specs=(vmem, vmem, vmem, hbm, hbm),
             scratch_shapes=[
-                scratch(2, Z, (2 * near + 1) * HALF + 16, LANES),
-                scratch(2, Z, HALF, size),
+                scratch(*pj_shape),
+                scratch(*a_shape),
                 scratch(2, 1, ROWS),
                 scratch(2, 8, LANES),
                 scratch(ROWS, size),
@@ -564,14 +599,30 @@
                 dma((2,)),
                 dma((2, 4)),
                 dma((2, 4)),
+                dma((2,)),
             ],
             compiler_params=pltpu.CompilerParams(
-                collective_id=0, has_side_effects=True, vmem_limit_bytes=48 * 2**20
+                collective_id=0, has_side_effects=True, vmem_limit_bytes=60 * 2**20
             ),
         )(elem_trans[0], elem_cov[0], elem_info[0], elem_mean, elem_infovec)
-        return lax.cond(
-            good[0, 0] > 0.5, lambda *_: (new_cov[None], new_mean), by_factors, *arrays
+        def otherwise(operands):
+            return pl.pallas_call(
+                functools.partial(return_kernel, T),
+                name="rows_to_owner",
+                out_shape=(struct(ROWS, size), struct(1, ROWS)),
+                in_specs=[vmem] * 4,
+                out_specs=(vmem, vmem),
+                scratch_shapes=[scratch(2, HALF, size), scratch(2, 8, LANES), dma((2, 2)), dma((2,))],
+                compiler_params=pltpu.CompilerParams(
+                    collective_id=1, has_side_effects=True, vmem_limit_bytes=16 * 2**20
+                ),
+            )(*by_factors(operands[:2]), operands[2], operands[3])
+
+        new_cov, new_mean = lax.cond(
+            good[0, 0] > 0.5, lambda *_: (new_cov, new_mean), lambda *operands: otherwise(operands),
+            pj, av, elem_cov[0], elem_mean,
         )
+        return new_cov[None], new_mean
 
     matrix, line = P("tm", "panel", None), P("tm", "panel")
     return jax.shard_map(

time: 104 us -> 92.1 us (0.89)
  between operations: 14.7 us -> 1.3 us
  Pallas kernels: 85.2 us -> 86.3 us
    pallas_call x1, Pallas kernels: 85.2 us -> 86.3 us  [body(): pl.pallas_call(functools.partial(solve_kernel, T, Z), name='gather_and_so...]
where the time goes in v3:
time: 92.1 us; the launch traced here: 91.8 us
  Pallas kernels  86.3 us (94%)
  local copies, waits for them, and re-layouts  4.03 us (4%)
  between operations  1.3 us (1%)
    pallas_call x1, Pallas kernels, body(): pl.pallas_call(functools.partial(solve_kernel, T, Z), name='gather_and_so...  86.3 us
    unnamed x2, local copies, waits for them, and re-layouts  2.85 us

profile of v3, /device:TPU:1, one launch (start us, length us, event | category | flops | bytes accessed | tf_op | source)
XLA Modules:
  0.0 91.8 jit_solution(837936284714727642)
XLA Ops:
  0.6 86.3 %gather_and_solve.1 = (f32[64,1024]{1,0:T(8,128)}, f32[1,64]{1,0:T(1,128)}, f32[8,128]{1,0:T(8,128)}, f32[2,16,304,128]{3,2,1,0:T(8,128)}, f32[2,16,32,1024]{3,2,1,0:T(8,128)}) custom-call(f32[64,1024]{1,0:T(8,128)} %bitcast.926, f32[64,1024]{1,0:T(8,128)} %bitcast.924, f32[64,1024]{1,0:T(8,128)} %bitcast.927, f32[1,64]{1,0:T(1,128)} %mean.1, f32[1,64]{1,0:T(1,128)} %infovec.1), custom_call_target="tpu_custom_call" | custom-call | tf_op jit(solution)/shard_map/gather_and_solve/pallas_call | solution.py:570
  86.9 1.2 %slice.580 = f32[1,1]{1,0:T(1,128)} slice(f32[8,128]{1,0:T(8,128)} %get-tuple-element.48), slice={[0:1], [0:1]} | slice | bytes 8 | tf_op jit(solution)/shard_map/slice | solution.py:622
  88.7 0.2 conditional.1
  89.0 1.7 %copy.789 = f32[1,64,1024]{2,1,0:T(8,128)} copy(f32[1,64,1024]{2,1,0:T(8,128)} %get-tuple-element.428) | data formatting | bytes 524288
  90.7 1.2 %copy.790 = f32[1,64]{1,0:T(1,128)} copy(f32[1,64]{1,0:T(1,128)} %get-tuple-element.429) | data formatting | bytes 512

commit v4 on v3

--- a/solution.py
+++ b/solution.py
@@ -352,9 +352,9 @@
     residual = target - x - exact(y, j_high, j_low)
     change = approximate(residual)
     x = x + change
-    moved = exact(change, p_high, p_low)
+    moved = dot(change.astype(BF16), p_high[...])
     y = y + moved
-    residual = residual - change - exact(moved, j_high, j_low)
+    residual = residual - change - dot(moved.astype(BF16), j_high[...])
     slow_result = agree(fast_result(), 1, chip_slow, slow_peers)
     while pending:
         next_hop()
@@ -404,7 +404,7 @@
     lax.fori_loop(1, H + 1, product_steps, 0)
     a_save = pltpu.make_async_copy(av, a_out, save.at[1])
     a_save.start()
-    good_out[...] = slow_result()
+    good_out[0] = jnp.min(slow_result())
     fetches[2].wait()
 
     @pl.when(low)
@@ -571,10 +571,10 @@
             functools.partial(solve_kernel, T, Z),
             name="gather_and_solve",
             out_shape=(
-                struct(ROWS, size), struct(1, ROWS), struct(8, LANES), struct(*pj_shape), struct(*a_shape)
+                struct(ROWS, size), struct(1, ROWS), struct(1), struct(*pj_shape), struct(*a_shape)
             ),
             in_specs=[hbm] * 5,
-            out_specs=(vmem, vmem, vmem, hbm, hbm),
+            out_specs=(vmem, vmem, pl.BlockSpec(memory_space=pltpu.SMEM), hbm, hbm),
             scratch_shapes=[
                 scratch(*pj_shape),
                 scratch(*a_shape),
@@ -619,7 +619,7 @@
             )(*by_factors(operands[:2]), operands[2], operands[3])
 
         new_cov, new_mean = lax.cond(
-            good[0, 0] > 0.5, lambda *_: (new_cov, new_mean), lambda *operands: otherwise(operands),
+            good[0] > 0.5, lambda *_: (new_cov, new_mean), lambda *operands: otherwise(operands),
             pj, av, elem_cov[0], elem_mean,
         )
         return new_cov[None], new_mean

time: 92.1 us -> 90.1 us (0.978)
  local copies, waits for them, and re-layouts: 4.03 us -> 2.85 us
    slice x1 -> x0, local copies, waits for them, and re-layouts: 1.19 us -> none  [body(): good[0, 0] > 0.5]
where the time goes in v4:
time: 90.1 us; the launch traced here: 89.9 us
  Pallas kernels  85.5 us (95%)
  local copies, waits for them, and re-layouts  2.85 us (3%)
  between operations  1.21 us (1%)
    pallas_call x1, Pallas kernels, body(): pl.pallas_call(functools.partial(solve_kernel, T, Z), name='gather_and_so...  85.5 us
    unnamed x2, local copies, waits for them, and re-layouts  2.85 us

profile of v4, /device:TPU:1, one launch (start us, length us, event | category | flops | bytes accessed | tf_op | source)
XLA Modules:
  0.0 89.9 jit_solution(16620459008756233275)
XLA Ops:
  0.6 85.5 %gather_and_solve.1 = (f32[64,1024]{1,0:T(8,128)}, f32[1,64]{1,0:T(1,128)}, f32[1]{0:T(128)}, f32[2,16,304,128]{3,2,1,0:T(8,128)}, f32[2,16,32,1024]{3,2,1,0:T(8,128)}) custom-call(f32[64,1024]{1,0:T(8,128)} %bitcast.926, f32[64,1024]{1,0:T(8,128)} %bitcast.924, f32[64,1024]{1,0:T(8,128)} %bitcast.927, f32[1,64]{1,0:T(1,128)} %mean.1, f32[1,64]{1,0:T(1,128)} %infovec.1), custom_call_target="tpu_custom_call" | custom-call | tf_op jit(solution)/shard_map/gather_and_solve/pallas_call | solution.py:570
  86.7 0.3 conditional.1
  87.0 1.7 %copy.789 = f32[1,64,1024]{2,1,0:T(8,128)} copy(f32[1,64,1024]{2,1,0:T(8,128)} %get-tuple-element.428) | data formatting | bytes 524288
  88.7 1.2 %copy.790 = f32[1,64]{1,0:T(1,128)} copy(f32[1,64]{1,0:T(1,128)} %get-tuple-element.429) | data formatting | bytes 512
